TPU v7x, 32 devices: a whole 2x2x4 slice. The times are simulated.
32 devices in a mesh: row: 8 (over y, x, core), col: 4 (over z).
Axes of the slice: x: 2, y: 2, z: 4, core: 2. Of those that a mesh axis runs over, the one named last changes fastest.
Arguments:
- row_frames: float32 [3, 1024, 256], P(None, ('row', 'col')), may hold values from -40 to 40, as said below
- col_frames: float32 [3, 1024, 256], P(None, ('col', 'row')), may hold values from -40 to 40, as said below
- vectors: float32 [64, 1024], P(None, ('col', 'row')), may hold values from -6 to 6
Outputs:
- embedding_product: float32 [64, 1024], P(None, ('row', 'col'))
Inputs may be any that keep to these rules, and one draw needn't show every extreme that they name: `row_frames`: frames of one chain of 256 atoms, each rigidly rotated and moved and perturbed by its own amount. `col_frames`: frames of one chain of 256 atoms, each rigidly rotated and moved and perturbed by its own amount.
All inputs are finite; a program needn't handle non-finite values.
Results may differ from a plain program's by a relative error of at most 0.00017.
Values sent between devices are 32-bit elements; how exact they have to be, the bound alone decides.
No kernel may reach another device: no remote copies, remote signals or barrier semaphores. Data moves between devices by JAX's collectives and lax.ppermute only.
A program may use at most 64 MiB of HBM per device.

v0:
```python
import functools

import jax
import jax.numpy as jnp
from jax import lax
from jax.experimental import pallas as pl
from jax.experimental.pallas import tpu as pltpu
from jax.sharding import PartitionSpec as P

NEWTON = 8
BAND = 2.0
LANES = 128
VM = pl.BlockSpec(memory_space=pltpu.VMEM)
NT = (((1,), (1,)), ((), ()))


def centre(frames):
    return frames - jnp.mean(frames, axis=-1, keepdims=True)


def split(x):
    high = x.astype(jnp.bfloat16)
    low = (x - high.astype(jnp.float32)).astype(jnp.bfloat16)
    return high, low


def pack(cols_ref, vec_ref, out_ref):
    comps, frames, atoms = cols_ref.shape
    nv = vec_ref.shape[1]
    for comp in range(comps):
        out_ref[comp * frames:(comp + 1) * frames, :] = centre(cols_ref[comp])
    out_ref[comps * frames:, :] = pack_vectors(vec_ref, atoms // nv)


def own_kernel(rows_ref, cols_ref, extra_ref, after_ref, near_ref, rows_out, packed_out):
    del after_ref, near_ref
    rows_out[...] = rows_ref[...]
    frames = cols_ref.shape[1]
    for comp in range(3):
        packed_out[comp * frames:(comp + 1) * frames, :] = centre(cols_ref[comp])
    packed_out[3 * frames:, :] = extra_ref[...]


def pack_vectors(vec_ref, groups):
    step = vec_ref.shape[0] // groups
    return jnp.concatenate([vec_ref[group * step:(group + 1) * step, :] for group in range(groups)], axis=1)


def vectors_kernel(vec_ref, out_ref):
    out_ref[...] = pack_vectors(vec_ref, out_ref.shape[1] // vec_ref.shape[1])


def after_first_kernel(extra_ref, first_cols_ref, first_vec_ref, far_ref, send_out, far_out):
    used = send_out.shape[0] - extra_ref.shape[0]
    pack(first_cols_ref, first_vec_ref, send_out.at[0:used])
    send_out[used:, :] = extra_ref[...]
    far_out[...] = far_ref[...]


def after_second_kernel(
    packed_ref, sent_ref, second_cols_ref, got_ref, own_ref, far_ref, near_ref, both_ref, blocks_out, rows_out
):
    used = packed_ref.shape[0]
    frames = second_cols_ref.shape[1]
    blocks_out[0] = packed_ref[...]
    blocks_out[1] = sent_ref[0:used, :]
    for comp in range(3):
        blocks_out[2, comp * frames:(comp + 1) * frames, :] = centre(second_cols_ref[comp])
    blocks_out[2, 3 * frames:, :] = got_ref[used:, :]
    blocks_out[3] = got_ref[0:used, :]
    for at, ref in enumerate((own_ref, far_ref, near_ref, both_ref)):
        rows_out[at] = ref[...]


def join_kernel(*refs):
    pairs = len(refs) // 3
    for at in range(pairs):
        first_ref, second_ref, out_ref = refs[2 * at], refs[2 * at + 1], refs[2 * pairs + at]
        count = first_ref.shape[0]
        out_ref[0:count] = first_ref[...]
        out_ref[count:] = second_ref[...]


def inverse(x):
    guess = pl.reciprocal(x, approx=True)
    return guess * (2.0 - x * guess)


def eigen_tile(m, half_norm, atoms):
    s00, s01, s02, s10, s11, s12, s20, s21, s22 = m
    coef_two = -2.0 * (
        s00 * s00 + s01 * s01 + s02 * s02 + s10 * s10 + s11 * s11 + s12 * s12 + s20 * s20 + s21 * s21 + s22 * s22
    )
    coef_one = 8.0 * (s00 * s12 * s21 + s11 * s20 * s02 + s22 * s01 * s10) - 8.0 * (
        s00 * s11 * s22 + s12 * s20 * s01 + s21 * s10 * s02
    )
    k00 = s00 + s11 + s22
    k11 = s00 - s11 - s22
    k22 = s11 - s00 - s22
    k33 = s22 - s00 - s11
    k01 = s12 - s21
    k02 = s20 - s02
    k03 = s01 - s10
    k12 = s01 + s10
    k13 = s20 + s02
    k23 = s12 + s21
    top0 = k00 * k11 - k01 * k01
    top1 = k00 * k12 - k01 * k02
    top2 = k00 * k13 - k01 * k03
    top3 = k01 * k12 - k11 * k02
    top4 = k01 * k13 - k11 * k03
    top5 = k02 * k13 - k12 * k03
    low0 = k02 * k13 - k03 * k12
    low1 = k02 * k23 - k03 * k22
    low2 = k02 * k33 - k03 * k23
    low3 = k12 * k23 - k13 * k22
    low4 = k12 * k33 - k13 * k23
    low5 = k22 * k33 - k23 * k23
    coef_zero = top0 * low5 - top1 * low4 + top2 * low3 + top3 * low2 - top4 * low1 + top5 * low0
    eigen = half_norm
    twice = coef_two + coef_two
    for _ in range(NEWTON):
        eigen_sq = eigen * eigen
        value = (eigen_sq + coef_two) * eigen_sq + coef_one * eigen + coef_zero
        slope = (4.0 * eigen_sq + twice) * eigen + coef_one
        eigen = eigen - value * inverse(slope)
    squared = jnp.maximum(2.0 * (half_norm - eigen) / atoms, 0.0)
    return jnp.exp(-squared / BAND)


def column_side(blocks_ref, frames, nv):
    count, _, atoms = blocks_ref.shape
    groups = atoms // nv
    step = frames // groups
    cols = [
        jnp.concatenate([blocks_ref[at, comp * frames:(comp + 1) * frames, :] for at in range(count)], axis=0)
        for comp in range(3)
    ]
    col_square = cols[0] * cols[0] + cols[1] * cols[1] + cols[2] * cols[2]
    norm = lax.dot_general(
        jnp.ones((8, atoms), jnp.float32), col_square, NT,
        precision=lax.Precision.HIGHEST, preferred_element_type=jnp.float32,
    )[0:1, :]
    high, low = split(jnp.concatenate(cols, axis=0))
    side = jnp.concatenate([high, high, low], axis=1)
    lane = lax.broadcasted_iota(jnp.int32, (step, LANES), 1)
    vec_parts = []
    for at in range(count):
        for group in range(groups):
            place = group * nv
            piece = blocks_ref[at, 3 * frames:, place // LANES * LANES:place // LANES * LANES + LANES]
            if place % LANES:
                piece = pltpu.roll(piece, LANES - place % LANES, 1)
            vec_parts.append(jnp.where(lane < nv, piece, jnp.where(lane == nv, 1.0, 0.0)))
    high, low = split(jnp.concatenate(vec_parts, axis=0))
    return side, norm, jnp.concatenate([high, high, low], axis=0)


def multiply(row_side, row_norm, side, norm, vec, atoms, moment, tile):
    count = row_norm.shape[0]
    count_cols = norm.shape[1]
    moment[...] = lax.dot_general(row_side, side, NT, preferred_element_type=jnp.float32)
    for at in range(0, count, 8):
        m = [
            moment[a * count + at:a * count + at + 8, b * count_cols:(b + 1) * count_cols]
            for a in range(3) for b in range(3)
        ]
        half_norm = 0.5 * (row_norm[at:at + 8, 0:1] + norm)
        tile[at:at + 8, :] = eigen_tile(m, half_norm, atoms)
    high, low = split(tile[...])
    return jnp.dot(jnp.concatenate([high, low, high], axis=1), vec, preferred_element_type=jnp.float32)


def first_kernel(nv, rows_ref, blocks_ref, sum_ref, side_ref, norm_ref, moment, tile):
    slots = [rows_ref.at[at] for at in range(rows_ref.shape[0])]
    _, frames, atoms = slots[0].shape
    groups, count, _ = sum_ref.shape
    side, norm, vec = column_side(blocks_ref, frames, nv)
    for group in range(groups):
        own = slots[group * count // frames:(group + 1) * count // frames]
        rows = [centre(jnp.concatenate([ref[comp] for ref in own], axis=0)) for comp in range(3)]
        square = jnp.sum(rows[0] * rows[0] + rows[1] * rows[1] + rows[2] * rows[2], axis=1, keepdims=True)
        row_norm = jnp.broadcast_to(square, (count, LANES))
        high, low = split(jnp.concatenate(rows, axis=0))
        row_side = jnp.concatenate([high, low, high], axis=1)
        side_ref[group] = row_side
        norm_ref[group] = row_norm
        sum_ref[group] = multiply(row_side, row_norm, side, norm, vec, atoms, moment, tile)


def second_kernel(nv, frames, sum_ref, side_ref, norm_ref, blocks_ref, *refs):
    moment, tile = refs[-2:]
    atoms = blocks_ref.shape[-1]
    groups, count, _ = sum_ref.shape
    side, norm, vec = column_side(blocks_ref, frames, nv)
    for group in range(groups):
        total = sum_ref[group] + multiply(side_ref[group], norm_ref[group], side, norm, vec, atoms, moment, tile)
        for at in range(count // frames):
            refs[group * count // frames + at][...] = total[at * frames:(at + 1) * frames, :]


def finish_kernel(nv, *refs):
    total = refs[0][...]
    for ref in refs[1:-1]:
        total = total + ref[...]
    refs[-1][...] = total[:, 0:nv] / total[:, nv:nv + 1]


def exchange(x, axis, mask, count):
    return lax.ppermute(x, axis, [(at, at ^ mask) for at in range(count)])


def call(kernel, outs, ins, name, scratch=(), megabytes=8, flops=0):
    out_shape = [jax.ShapeDtypeStruct(*out) for out in outs]
    moved = sum(x.size * 4 for x in ins)
    return pl.pallas_call(
        kernel,
        out_shape=out_shape,
        in_specs=[VM] * len(ins),
        out_specs=[VM] * len(outs),
        scratch_shapes=list(scratch),
        compiler_params=pltpu.CompilerParams(vmem_limit_bytes=megabytes * 1024 * 1024),
        cost_estimate=pl.CostEstimate(flops=flops, bytes_accessed=moved, transcendentals=0),
        name=name,
    )(*ins)


def per_device(n_row, n_col, row_frames, col_frames, vectors):
    comps, frames, atoms = row_frames.shape
    nv = vectors.shape[0]
    f32, bf16 = jnp.float32, jnp.bfloat16
    vec_own = vectors.T
    row_masks = [n_col >> at for at in range(1, n_col.bit_length())]
    col_masks = [1 << at for at in range(1, n_row.bit_length() - 1)]

    far = exchange(row_frames, "col", row_masks[0], n_col)
    first_cols = exchange(col_frames, "row", col_masks[0], n_row)
    second_cols = exchange(col_frames, "row", col_masks[1], n_row)
    near = exchange(row_frames, "col", row_masks[1], n_col)
    first_vec = exchange(vec_own, "row", col_masks[0], n_row)
    extra = frames * nv // atoms
    packed_shape = (comps * frames + extra, atoms)
    (own_extra,) = call(vectors_kernel, [((extra, atoms), f32)], [vec_own], "vectors", flops=1 << 30)
    onward, far = call(
        after_first_kernel,
        [((packed_shape[0] + extra, atoms), f32), (row_frames.shape, f32)],
        [own_extra, first_cols, first_vec, far], "after_first",
    )
    both = exchange(far, "col", row_masks[1], n_col)
    xy = exchange(onward, "row", col_masks[1], n_row)
    own, packed = call(
        own_kernel, [(row_frames.shape, f32), (packed_shape, f32)], [row_frames, col_frames, own_extra, far, near], "own",
        flops=1 << 30,
    )
    blocks, rows = call(
        after_second_kernel, [((4, *packed_shape), f32), ((4, *row_frames.shape), f32)],
        [packed, onward, second_cols, xy, own, far, near, both], "after_second",
    )
    order = [0, row_masks[0], row_masks[1], row_masks[0] ^ row_masks[1]]
    for at in range(2, max(len(row_masks), len(col_masks))):
        joins = []
        if at < len(row_masks):
            joins += [rows, exchange(rows, "col", row_masks[at], n_col)]
            order = order + [row_masks[at] ^ slot for slot in order]
        if at < len(col_masks):
            joins += [blocks, exchange(blocks, "row", col_masks[at], n_row)]
        joined = call(join_kernel, [((2 * x.shape[0], *x.shape[1:]), f32) for x in joins[::2]], joins, "join")
        if at < len(col_masks):
            blocks = joined[-1]
        if at < len(row_masks):
            rows = joined[0]
    other = exchange(blocks, "row", 1, n_row)

    half_cols = n_row // 2 * frames
    count = min(n_col, max(1, LANES // frames)) * frames
    groups = n_col * frames // count
    scratch = [pltpu.VMEM((3 * count, 3 * half_cols), f32), pltpu.VMEM((count, half_cols), f32)]
    work = 2 * 3 * n_col * frames * 3 * half_cols * 3 * atoms
    sums, side, norm = call(
        functools.partial(first_kernel, nv),
        [((groups, count, LANES), f32), ((groups, 3 * count, 3 * atoms), bf16), ((groups, count, LANES), f32)],
        [rows, blocks], "first_tile", scratch, 32, work,
    )
    parts = call(
        functools.partial(second_kernel, nv, frames), [((frames, LANES), f32)] * n_col,
        [sums, side, norm, other], "second_tile", scratch, 32, work,
    )
    shares = [parts[0]] + [
        exchange(parts[order.index(mask)], "col", mask, n_col) for mask in range(n_col - 1, 0, -1)
    ]
    (result,) = call(functools.partial(finish_kernel, nv), [((frames, nv), f32)], shares, "sum_divide")
    return result.T


def solution(mesh):
    return jax.shard_map(
        functools.partial(per_device, mesh.shape["row"], mesh.shape["col"]),
        mesh=mesh,
        in_specs=(
            P(None, ("row", "col"), None),
            P(None, ("col", "row"), None),
            P(None, ("col", "row")),
        ),
        out_specs=P(None, ("row", "col")),
        check_vma=False,
    )
```

profile of v0, /device:TPU:0, one launch (start us, length us, event | category | flops | bytes accessed | tf_op | source)
XLA Modules:
  0.0 28.8 jit_solution(12133412229564334551)
XLA Ops:
  0.0 4.0 %collective-permute-start.2 = (f32[3,32,256]{2,1,0:T(8,128)}, f32[3,32,256]{2,1,0:T(8,128)S(1)}, u32[]{:S(2)}, u32[]{:S(2)}) collective-permute-start(f32[3,32,256]{2,1,0:T(8,128)} %rows_ref.1), channel_id=1, source_target_pairs={{0,2},{1,3},{2,0},{3,1},{4,6},{5,7},{6,4},{7,5},{8,10},{9,11},{10,... | collective-permute-start | bytes 294920 | tf_op jit(solution)/shard_map/ppermute | solution.py:210
  4.0 1.6 %collective-permute-start.3 = (f32[3,32,256]{2,1,0:T(8,128)}, f32[3,32,256]{2,1,0:T(8,128)S(1)}, u32[]{:S(2)}, u32[]{:S(2)}) collective-permute-start(f32[3,32,256]{2,1,0:T(8,128)} %rows_ref.1), channel_id=1, source_target_pairs={{0,1},{1,0},{2,3},{3,2},{4,5},{5,4},{6,7},{7,6},{8,9},{9,8},{10,11... | collective-permute-start | bytes 294920 | tf_op jit(solution)/shard_map/ppermute | solution.py:210
  5.6 1.5 %collective-permute-start.1 = (f32[32,64]{1,0:T(8,128)}, f32[32,64]{1,0:T(8,128)S(1)}, u32[]{:S(2)}, u32[]{:S(2)}) collective-permute-start(f32[32,64]{1,0:T(8,128)} %bitcast.2), channel_id=1, source_target_pairs={{0,8},{4,12},{8,0},{12,4},{16,24},{20,28},{24,16},{28,20},{1,9},{5... | collective-permute-start | bytes 24584 | tf_op jit(solution)/shard_map/ppermute | solution.py:210
  7.1 0.5 %collective-permute-start = (f32[3,32,256]{2,1,0:T(8,128)}, f32[3,32,256]{2,1,0:T(8,128)S(1)}, u32[]{:S(2)}, u32[]{:S(2)}) collective-permute-start(f32[3,32,256]{2,1,0:T(8,128)} %cols_ref.1), channel_id=1, source_target_pairs={{0,8},{4,12},{8,0},{12,4},{16,24},{20,28},{24,16},{28,20},{1,9},{5... | collective-permute-start | bytes 294920 | tf_op jit(solution)/shard_map/ppermute | solution.py:210
  7.6 0.7 %copy-done.2 = f32[64,32]{0,1:T(8,128)S(1)} copy-done((f32[64,32]{0,1:T(8,128)S(1)}, f32[64,32]{0,1:T(8,128)}, u32[]{:S(2)}) %copy-start.2) | copy-done | bytes 8216
  8.4 0.1 vectors.1.extra_ref
  8.4 1.2 %collective-permute-done.1.first_vec_ref = f32[32,64]{1,0:T(8,128)S(1)} collective-permute-done((f32[32,64]{1,0:T(8,128)}, f32[32,64]{1,0:T(8,128)S(1)}, u32[]{:S(2)}, u32[]{:S(2)}) %collective-permute-start.1) | collective-permute-done | bytes 8224 | tf_op jit(solution)/shard_map/ppermute | solution.py:210
  9.7 0.0 collective-permute-done.2.far_ref
  9.7 2.3 %collective-permute-done.first_cols_ref = f32[3,32,256]{2,1,0:T(8,128)S(1)} collective-permute-done((f32[3,32,256]{2,1,0:T(8,128)}, f32[3,32,256]{2,1,0:T(8,128)S(1)}, u32[]{:S(2)}, u32[]{:S(2)}) %collective-permute-start) | collective-permute-done | bytes 98336 | tf_op jit(solution)/shard_map/ppermute | solution.py:210
  11.9 0.1 after_first.1
  12.0 1.6 %collective-permute-start.5 = (f32[112,256]{1,0:T(8,128)S(1)}, f32[112,256]{1,0:T(8,128)S(1)}, u32[]{:S(2)}, u32[]{:S(2)}) collective-permute-start(f32[112,256]{1,0:T(8,128)S(1)} %get-tuple-element.20.sent_ref), channel_id=1, source_target_pairs={{0,16},{4,20},{8,24},{12,28},{16,0},{20,4},{24,8},{28,12},{1,17},{... | collective-permute-start | bytes 344072 | tf_op jit(solution)/shard_map/ppermute | solution.py:210
  13.6 0.0 copy-done.1
  13.6 0.5 %collective-permute-start.4 = (f32[3,32,256]{2,1,0:T(8,128)S(1)}, f32[3,32,256]{2,1,0:T(8,128)S(1)}, u32[]{:S(2)}, u32[]{:S(2)}) collective-permute-start(f32[3,32,256]{2,1,0:T(8,128)S(1)} %copy-done.1), channel_id=1, source_target_pairs={{0,16},{4,20},{8,24},{12,28},{16,0},{20,4},{24,8},{28,12},{1,17},{... | collective-permute-start | bytes 294920 | tf_op jit(solution)/shard_map/ppermute | solution.py:210
  14.1 0.4 %collective-permute-start.6 = (f32[3,32,256]{2,1,0:T(8,128)S(1)}, f32[3,32,256]{2,1,0:T(8,128)S(1)}, u32[]{:S(2)}, u32[]{:S(2)}) collective-permute-start(f32[3,32,256]{2,1,0:T(8,128)S(1)} %get-tuple-element.18.after_ref.far_ref), channel_id=1, source_target_pairs={{0,1},{1,0},{2,3},{3,2},{4,5},{5,4},{6,7},{7,6},{8,9},{9,8},{10,11... | collective-permute-start | bytes 294920 | tf_op jit(solution)/shard_map/ppermute | solution.py:210
  14.6 0.0 collective-permute-done.3.near_ref
  14.6 0.0 copy-done
  14.6 0.1 own.1
  14.7 3.6 %collective-permute-done.4.second_cols_ref = f32[3,32,256]{2,1,0:T(8,128)S(1)} collective-permute-done((f32[3,32,256]{2,1,0:T(8,128)S(1)}, f32[3,32,256]{2,1,0:T(8,128)S(1)}, u32[]{:S(2)}, u32[]{:S(2)}) %collective-permute-start.4) | collective-permute-done | bytes 98336 | tf_op jit(solution)/shard_map/ppermute | solution.py:210
  18.2 0.5 %collective-permute-done.6.both_ref = f32[3,32,256]{2,1,0:T(8,128)S(1)} collective-permute-done((f32[3,32,256]{2,1,0:T(8,128)S(1)}, f32[3,32,256]{2,1,0:T(8,128)S(1)}, u32[]{:S(2)}, u32[]{:S(2)}) %collective-permute-start.6) | collective-permute-done | bytes 98336 | tf_op jit(solution)/shard_map/ppermute | solution.py:210
  18.7 0.0 collective-permute-done.5.got_ref
  18.7 0.1 after_second.1
  18.8 0.1 collective-permute-start.7
  18.9 1.2 %first_tile.1 = (f32[1,128,128]{2,1,0:T(8,128)S(1)}, bf16[1,384,768]{2,1,0:T(8,128)(2,1)S(1)}, f32[1,128,128]{2,1,0:T(8,128)S(1)}) custom-call(f32[4,3,32,256]{3,2,1,0:T(8,128)S(1)} %get-tuple-element.22.rows_ref, f32[4,104,256]{2,1,0:T(8,128)S(1)} %get-tuple-element.23.blocks_ref), custom_call_target="tpu_custom_call" | custom-call | flops 226492416 | bytes 819200 | tf_op jit(solution)/shard_map/first_tile/pallas_call | solution.py:216
  20.2 0.5 %collective-permute-done.7.blocks_ref = f32[4,104,256]{2,1,0:T(8,128)S(1)} collective-permute-done((f32[4,104,256]{2,1,0:T(8,128)S(1)}, f32[4,104,256]{2,1,0:T(8,128)S(1)}, u32[]{:S(2)}, u32[]{:S(2)}) %collective-permute-start.7) | collective-permute-done | bytes 426016 | tf_op jit(solution)/shard_map/ppermute | solution.py:210
  20.7 1.2 %second_tile.1 = (f32[32,128]{1,0:T(8,128)S(1)}, f32[32,128]{1,0:T(8,128)S(1)}, f32[32,128]{1,0:T(8,128)S(1)}, f32[32,128]{1,0:T(8,128)S(1)}) custom-call(f32[1,128,128]{2,1,0:T(8,128)S(1)} %get-tuple-element.24.sum_ref, bf16[1,384,768]{2,1,0:T(8,128)(2,1)S(1)} %get-tuple-element.25.side_ref, f32[1,128,128]{2,1,0:T(8,128)S(1)} %get-tuple-element.26.norm_ref, ...), custom_call_target="tpu_custom_call" | custom-call | flops 226492416 | bytes 1736704 | tf_op jit(solution)/shard_map/second_tile/pallas_call | solution.py:216
  21.9 1.4 %collective-permute-start.8 = (f32[32,128]{1,0:T(8,128)S(1)}, f32[32,128]{1,0:T(8,128)S(1)}, u32[]{:S(2)}, u32[]{:S(2)}) collective-permute-start(f32[32,128]{1,0:T(8,128)S(1)} %get-tuple-element.28), channel_id=1, source_target_pairs={{0,3},{1,2},{2,1},{3,0},{4,7},{5,6},{6,5},{7,4},{8,11},{9,10},{10,... | collective-permute-start | bytes 49160 | tf_op jit(solution)/shard_map/ppermute | solution.py:210
  23.3 0.6 %collective-permute-start.9 = (f32[32,128]{1,0:T(8,128)S(1)}, f32[32,128]{1,0:T(8,128)S(1)}, u32[]{:S(2)}, u32[]{:S(2)}) collective-permute-start(f32[32,128]{1,0:T(8,128)S(1)} %get-tuple-element.29), channel_id=1, source_target_pairs={{0,2},{1,3},{2,0},{3,1},{4,6},{5,7},{6,4},{7,5},{8,10},{9,11},{10,... | collective-permute-start | bytes 49160 | tf_op jit(solution)/shard_map/ppermute | solution.py:210
  23.9 2.5 %collective-permute-start.10 = (f32[32,128]{1,0:T(8,128)S(1)}, f32[32,128]{1,0:T(8,128)S(1)}, u32[]{:S(2)}, u32[]{:S(2)}) collective-permute-start(f32[32,128]{1,0:T(8,128)S(1)} %get-tuple-element.30), channel_id=1, source_target_pairs={{0,1},{1,0},{2,3},{3,2},{4,5},{5,4},{6,7},{7,6},{8,9},{9,8},{10,11... | collective-permute-start | bytes 49160 | tf_op jit(solution)/shard_map/ppermute | solution.py:210
  26.4 1.1 %collective-permute-done.8.refs_1_ = f32[32,128]{1,0:T(8,128)S(1)} collective-permute-done((f32[32,128]{1,0:T(8,128)S(1)}, f32[32,128]{1,0:T(8,128)S(1)}, u32[]{:S(2)}, u32[]{:S(2)}) %collective-permute-start.8) | collective-permute-done | bytes 16416 | tf_op jit(solution)/shard_map/ppermute | solution.py:210
  27.5 0.4 %collective-permute-done.9.refs_2_ = f32[32,128]{1,0:T(8,128)S(1)} collective-permute-done((f32[32,128]{1,0:T(8,128)S(1)}, f32[32,128]{1,0:T(8,128)S(1)}, u32[]{:S(2)}, u32[]{:S(2)}) %collective-permute-start.9) | collective-permute-done | bytes 16416 | tf_op jit(solution)/shard_map/ppermute | solution.py:210
  27.9 0.2 collective-permute-done.10.refs_3_
  28.1 0.7 %sum_divide.1 = f32[32,64]{1,0:T(8,128)} custom-call(f32[32,128]{1,0:T(8,128)S(1)} %get-tuple-element.27.refs_0_, f32[32,128]{1,0:T(8,128)S(1)} %collective-permute-done.8.refs_1_, f32[32,128]{1,0:T(8,128)S(1)} %collective-permute-done.9.refs_2_, f32[32,128]{1,0:T(8,128)S(1)} %collective-permute-done.10.refs_3_), custom_call_target="tpu_custom_call" | custom-call | bytes 65536 | tf_op jit(solution)/shard_map/sum_divide/pallas_call | solution.py:216
  (3 shorter events, 0.0 us)
Async XLA Ops:
  0.0 9.7 %collective-permute-start.2 = (f32[3,32,256]{2,1,0:T(8,128)}, f32[3,32,256]{2,1,0:T(8,128)S(1)}, u32[]{:S(2)}, u32[]{:S(2)}) collective-permute-start(f32[3,32,256]{2,1,0:T(8,128)} %rows_ref.1), channel_id=1, source_target_pairs={{0,2},{1,3},{2,0},{3,1},{4,6},{5,7},{6,4},{7,5},{8,10},{9,11},{10,... | collective-permute-start | bytes 294920 | tf_op jit(solution)/shard_map/ppermute | solution.py:210
  4.0 10.5 %collective-permute-start.3 = (f32[3,32,256]{2,1,0:T(8,128)}, f32[3,32,256]{2,1,0:T(8,128)S(1)}, u32[]{:S(2)}, u32[]{:S(2)}) collective-permute-start(f32[3,32,256]{2,1,0:T(8,128)} %rows_ref.1), channel_id=1, source_target_pairs={{0,1},{1,0},{2,3},{3,2},{4,5},{5,4},{6,7},{7,6},{8,9},{9,8},{10,11... | collective-permute-start | bytes 294920 | tf_op jit(solution)/shard_map/ppermute | solution.py:210
  5.6 4.0 %collective-permute-start.1 = (f32[32,64]{1,0:T(8,128)}, f32[32,64]{1,0:T(8,128)S(1)}, u32[]{:S(2)}, u32[]{:S(2)}) collective-permute-start(f32[32,64]{1,0:T(8,128)} %bitcast.2), channel_id=1, source_target_pairs={{0,8},{4,12},{8,0},{12,4},{16,24},{20,28},{24,16},{28,20},{1,9},{5... | collective-permute-start | bytes 24584 | tf_op jit(solution)/shard_map/ppermute | solution.py:210
  7.1 4.8 %collective-permute-start = (f32[3,32,256]{2,1,0:T(8,128)}, f32[3,32,256]{2,1,0:T(8,128)S(1)}, u32[]{:S(2)}, u32[]{:S(2)}) collective-permute-start(f32[3,32,256]{2,1,0:T(8,128)} %cols_ref.1), channel_id=1, source_target_pairs={{0,8},{4,12},{8,0},{12,4},{16,24},{20,28},{24,16},{28,20},{1,9},{5... | collective-permute-start | bytes 294920 | tf_op jit(solution)/shard_map/ppermute | solution.py:210
  7.6 0.7 %copy-start.2 = (f32[64,32]{0,1:T(8,128)S(1)}, f32[64,32]{0,1:T(8,128)}, u32[]{:S(2)}) copy-start(f32[64,32]{0,1:T(8,128)} %param.5) | copy-start | bytes 24580
  8.4 5.2 %copy-start.1 = (f32[3,32,256]{2,1,0:T(8,128)S(1)}, f32[3,32,256]{2,1,0:T(8,128)}, u32[]{:S(2)}) copy-start(f32[3,32,256]{2,1,0:T(8,128)} %cols_ref.1) | copy-start | bytes 294916
  8.4 6.1 %copy-start = (f32[3,32,256]{2,1,0:T(8,128)S(1)}, f32[3,32,256]{2,1,0:T(8,128)}, u32[]{:S(2)}) copy-start(f32[3,32,256]{2,1,0:T(8,128)} %rows_ref.1) | copy-start | bytes 294916
  12.0 6.7 %collective-permute-start.5 = (f32[112,256]{1,0:T(8,128)S(1)}, f32[112,256]{1,0:T(8,128)S(1)}, u32[]{:S(2)}, u32[]{:S(2)}) collective-permute-start(f32[112,256]{1,0:T(8,128)S(1)} %get-tuple-element.20.sent_ref), channel_id=1, source_target_pairs={{0,16},{4,20},{8,24},{12,28},{16,0},{20,4},{24,8},{28,12},{1,17},{... | collective-permute-start | bytes 344072 | tf_op jit(solution)/shard_map/ppermute | solution.py:210
  13.6 4.6 %collective-permute-start.4 = (f32[3,32,256]{2,1,0:T(8,128)S(1)}, f32[3,32,256]{2,1,0:T(8,128)S(1)}, u32[]{:S(2)}, u32[]{:S(2)}) collective-permute-start(f32[3,32,256]{2,1,0:T(8,128)S(1)} %copy-done.1), channel_id=1, source_target_pairs={{0,16},{4,20},{8,24},{12,28},{16,0},{20,4},{24,8},{28,12},{1,17},{... | collective-permute-start | bytes 294920 | tf_op jit(solution)/shard_map/ppermute | solution.py:210
  14.1 4.6 %collective-permute-start.6 = (f32[3,32,256]{2,1,0:T(8,128)S(1)}, f32[3,32,256]{2,1,0:T(8,128)S(1)}, u32[]{:S(2)}, u32[]{:S(2)}) collective-permute-start(f32[3,32,256]{2,1,0:T(8,128)S(1)} %get-tuple-element.18.after_ref.far_ref), channel_id=1, source_target_pairs={{0,1},{1,0},{2,3},{3,2},{4,5},{5,4},{6,7},{7,6},{8,9},{9,8},{10,11... | collective-permute-start | bytes 294920 | tf_op jit(solution)/shard_map/ppermute | solution.py:210
  18.8 1.8 %collective-permute-start.7 = (f32[4,104,256]{2,1,0:T(8,128)S(1)}, f32[4,104,256]{2,1,0:T(8,128)S(1)}, u32[]{:S(2)}, u32[]{:S(2)}) collective-permute-start(f32[4,104,256]{2,1,0:T(8,128)S(1)} %get-tuple-element.23.blocks_ref), channel_id=1, source_target_pairs={{0,4},{4,0},{8,12},{12,8},{16,20},{20,16},{24,28},{28,24},{1,5},{5... | collective-permute-start | bytes 1277960 | tf_op jit(solution)/shard_map/ppermute | solution.py:210
  21.9 5.6 %collective-permute-start.8 = (f32[32,128]{1,0:T(8,128)S(1)}, f32[32,128]{1,0:T(8,128)S(1)}, u32[]{:S(2)}, u32[]{:S(2)}) collective-permute-start(f32[32,128]{1,0:T(8,128)S(1)} %get-tuple-element.28), channel_id=1, source_target_pairs={{0,3},{1,2},{2,1},{3,0},{4,7},{5,6},{6,5},{7,4},{8,11},{9,10},{10,... | collective-permute-start | bytes 49160 | tf_op jit(solution)/shard_map/ppermute | solution.py:210
  23.3 4.6 %collective-permute-start.9 = (f32[32,128]{1,0:T(8,128)S(1)}, f32[32,128]{1,0:T(8,128)S(1)}, u32[]{:S(2)}, u32[]{:S(2)}) collective-permute-start(f32[32,128]{1,0:T(8,128)S(1)} %get-tuple-element.29), channel_id=1, source_target_pairs={{0,2},{1,3},{2,0},{3,1},{4,6},{5,7},{6,4},{7,5},{8,10},{9,11},{10,... | collective-permute-start | bytes 49160 | tf_op jit(solution)/shard_map/ppermute | solution.py:210
  23.9 4.2 %collective-permute-start.10 = (f32[32,128]{1,0:T(8,128)S(1)}, f32[32,128]{1,0:T(8,128)S(1)}, u32[]{:S(2)}, u32[]{:S(2)}) collective-permute-start(f32[32,128]{1,0:T(8,128)S(1)} %get-tuple-element.30), channel_id=1, source_target_pairs={{0,1},{1,0},{2,3},{3,2},{4,5},{5,4},{6,7},{7,6},{8,9},{9,8},{10,11... | collective-permute-start | bytes 49160 | tf_op jit(solution)/shard_map/ppermute | solution.py:210
where the time goes:
time: 29 us; the launch traced here: 28.8 us
  starting transfers between devices  14.7 us (51%)
  waiting for transfers between devices  9.78 us (34%)
  Pallas kernels  3.51 us (12%)
  local copies, waits for them, and re-layouts  0.72 us (2%)
    ppermute x11, starting transfers between devices, exchange(): return lax.ppermute(x, axis, [(at, at ^ mask) for at in range(count)])  14.7 us
    ppermute x11, waiting for transfers between devices, exchange(): return lax.ppermute(x, axis, [(at, at ^ mask) for at in range(count)])  9.78 us
    pallas_call x7, Pallas kernels, call(): pl.pallas_call(kernel, out_shape=out_shape, in_specs=[VM] * len(ins), out...  3.51 us
    unnamed x6, local copies, waits for them, and re-layouts  0.72 us
  transfers between devices with their start and end apart: 11, of which 8 were waited for; matrix products, arithmetic and copies ran while one was open for 0% of the time, Pallas kernels for 5%

commit v1 on v0

--- a/solution.py
+++ b/solution.py
@@ -24,16 +24,8 @@
     return high, low
 
 
-def pack(cols_ref, vec_ref, out_ref):
-    comps, frames, atoms = cols_ref.shape
-    nv = vec_ref.shape[1]
-    for comp in range(comps):
-        out_ref[comp * frames:(comp + 1) * frames, :] = centre(cols_ref[comp])
-    out_ref[comps * frames:, :] = pack_vectors(vec_ref, atoms // nv)
-
-
-def own_kernel(rows_ref, cols_ref, extra_ref, after_ref, near_ref, rows_out, packed_out):
-    del after_ref, near_ref
+def own_kernel(rows_ref, cols_ref, extra_ref, after_ref, second_cols_ref, near_ref, rows_out, packed_out):
+    del after_ref, second_cols_ref, near_ref
     rows_out[...] = rows_ref[...]
     frames = cols_ref.shape[1]
     for comp in range(3):
@@ -50,24 +42,29 @@
     out_ref[...] = pack_vectors(vec_ref, out_ref.shape[1] // vec_ref.shape[1])
 
 
-def after_first_kernel(extra_ref, first_cols_ref, first_vec_ref, far_ref, send_out, far_out):
-    used = send_out.shape[0] - extra_ref.shape[0]
-    pack(first_cols_ref, first_vec_ref, send_out.at[0:used])
-    send_out[used:, :] = extra_ref[...]
+def after_first_kernel(extra_ref, cols_ref, far_ref, send_out, far_out):
+    frames = cols_ref.shape[1]
+    for comp in range(3):
+        send_out[comp * frames:(comp + 1) * frames, :] = centre(cols_ref[comp])
+    send_out[3 * frames:, :] = extra_ref[...]
     far_out[...] = far_ref[...]
 
 
 def after_second_kernel(
-    packed_ref, sent_ref, second_cols_ref, got_ref, own_ref, far_ref, near_ref, both_ref, blocks_out, rows_out
+    packed_ref, sent_ref, second_cols_ref, got_ref, first_vec_ref, both_vec_ref,
+    own_ref, far_ref, near_ref, both_ref, blocks_out, rows_out
 ):
-    used = packed_ref.shape[0]
     frames = second_cols_ref.shape[1]
+    used = 3 * frames
+    groups = packed_ref.shape[1] // first_vec_ref.shape[1]
     blocks_out[0] = packed_ref[...]
-    blocks_out[1] = sent_ref[0:used, :]
+    blocks_out[1, 0:used, :] = sent_ref[0:used, :]
+    blocks_out[1, used:, :] = pack_vectors(first_vec_ref, groups)
     for comp in range(3):
         blocks_out[2, comp * frames:(comp + 1) * frames, :] = centre(second_cols_ref[comp])
-    blocks_out[2, 3 * frames:, :] = got_ref[used:, :]
-    blocks_out[3] = got_ref[0:used, :]
+    blocks_out[2, used:, :] = got_ref[used:, :]
+    blocks_out[3, 0:used, :] = got_ref[0:used, :]
+    blocks_out[3, used:, :] = pack_vectors(both_vec_ref, groups)
     for at, ref in enumerate((own_ref, far_ref, near_ref, both_ref)):
         rows_out[at] = ref[...]
 
@@ -233,28 +230,27 @@
     row_masks = [n_col >> at for at in range(1, n_col.bit_length())]
     col_masks = [1 << at for at in range(1, n_row.bit_length() - 1)]
 
+    extra = frames * nv // atoms
+    packed_shape = (comps * frames + extra, atoms)
     far = exchange(row_frames, "col", row_masks[0], n_col)
+    near = exchange(row_frames, "col", row_masks[1], n_col)
     first_cols = exchange(col_frames, "row", col_masks[0], n_row)
     second_cols = exchange(col_frames, "row", col_masks[1], n_row)
-    near = exchange(row_frames, "col", row_masks[1], n_col)
     first_vec = exchange(vec_own, "row", col_masks[0], n_row)
-    extra = frames * nv // atoms
-    packed_shape = (comps * frames + extra, atoms)
     (own_extra,) = call(vectors_kernel, [((extra, atoms), f32)], [vec_own], "vectors", flops=1 << 30)
     onward, far = call(
-        after_first_kernel,
-        [((packed_shape[0] + extra, atoms), f32), (row_frames.shape, f32)],
-        [own_extra, first_cols, first_vec, far], "after_first",
+        after_first_kernel, [(packed_shape, f32), (row_frames.shape, f32)], [own_extra, first_cols, far], "after_first"
     )
     both = exchange(far, "col", row_masks[1], n_col)
-    xy = exchange(onward, "row", col_masks[1], n_row)
+    got = exchange(onward, "row", col_masks[1], n_row)
+    both_vec = exchange(first_vec, "row", col_masks[1], n_row)
     own, packed = call(
-        own_kernel, [(row_frames.shape, f32), (packed_shape, f32)], [row_frames, col_frames, own_extra, far, near], "own",
-        flops=1 << 30,
+        own_kernel, [(row_frames.shape, f32), (packed_shape, f32)],
+        [row_frames, col_frames, own_extra, far, second_cols, near], "own", flops=1 << 30,
     )
     blocks, rows = call(
         after_second_kernel, [((4, *packed_shape), f32), ((4, *row_frames.shape), f32)],
-        [packed, onward, second_cols, xy, own, far, near, both], "after_second",
+        [packed, onward, second_cols, got, first_vec, both_vec, own, far, near, both], "after_second",
     )
     order = [0, row_masks[0], row_masks[1], row_masks[0] ^ row_masks[1]]
     for at in range(2, max(len(row_masks), len(col_masks))):

time: 29 us -> 28.3 us (0.976)
  waiting for transfers between devices: 9.78 us -> 7.69 us
  starting transfers between devices: 14.7 us -> 16 us
    ppermute x11 -> x12, waiting for transfers between devices: 9.78 us -> 7.69 us  [exchange(): return lax.ppermute(x, axis, [(at, at ^ mask) for at in range(count)])]
    ppermute x11 -> x12, starting transfers between devices: 14.7 us -> 16 us  [exchange(): return lax.ppermute(x, axis, [(at, at ^ mask) for at in range(count)])]
  transfers between devices with their start and end apart: 11 -> 12, of which waited for: 8 -> 7; matrix products, arithmetic and copies ran while one was open for 0% -> 0% of each run, Pallas kernels for 5% -> 5%
where the time goes in v1:
time: 28.3 us; the launch traced here: 28.1 us
  starting transfers between devices  16 us (57%)
  waiting for transfers between devices  7.69 us (27%)
  Pallas kernels  3.52 us (12%)
  local copies, waits for them, and re-layouts  0.76 us (3%)
    ppermute x12, starting transfers between devices, exchange(): return lax.ppermute(x, axis, [(at, at ^ mask) for at in range(count)])  16 us
    ppermute x12, waiting for transfers between devices, exchange(): return lax.ppermute(x, axis, [(at, at ^ mask) for at in range(count)])  7.69 us
    pallas_call x7, Pallas kernels, call(): pl.pallas_call(kernel, out_shape=out_shape, in_specs=[VM] * len(ins), out...  3.52 us
    unnamed x6, local copies, waits for them, and re-layouts  0.76 us
  transfers between devices with their start and end apart: 12, of which 7 were waited for; matrix products, arithmetic and copies ran while one was open for 0% of the time, Pallas kernels for 5%

profile of v1, /device:TPU:0, one launch (start us, length us, event | category | flops | bytes accessed | tf_op | source)
XLA Modules:
  0.0 28.1 jit_solution(5871433203378428657)
XLA Ops:
  0.0 4.0 %collective-permute-start.1 = (f32[3,32,256]{2,1,0:T(8,128)}, f32[3,32,256]{2,1,0:T(8,128)S(1)}, u32[]{:S(2)}, u32[]{:S(2)}) collective-permute-start(f32[3,32,256]{2,1,0:T(8,128)} %rows_ref.1), channel_id=1, source_target_pairs={{0,2},{1,3},{2,0},{3,1},{4,6},{5,7},{6,4},{7,5},{8,10},{9,11},{10,... | collective-permute-start | bytes 294920 | tf_op jit(solution)/shard_map/ppermute | solution.py:207
  4.0 1.6 %collective-permute-start.3 = (f32[3,32,256]{2,1,0:T(8,128)}, f32[3,32,256]{2,1,0:T(8,128)S(1)}, u32[]{:S(2)}, u32[]{:S(2)}) collective-permute-start(f32[3,32,256]{2,1,0:T(8,128)} %rows_ref.1), channel_id=1, source_target_pairs={{0,1},{1,0},{2,3},{3,2},{4,5},{5,4},{6,7},{7,6},{8,9},{9,8},{10,11... | collective-permute-start | bytes 294920 | tf_op jit(solution)/shard_map/ppermute | solution.py:207
  5.6 1.5 %collective-permute-start = (f32[3,32,256]{2,1,0:T(8,128)}, f32[3,32,256]{2,1,0:T(8,128)S(1)}, u32[]{:S(2)}, u32[]{:S(2)}) collective-permute-start(f32[3,32,256]{2,1,0:T(8,128)} %cols_ref.1), channel_id=1, source_target_pairs={{0,8},{4,12},{8,0},{12,4},{16,24},{20,28},{24,16},{28,20},{1,9},{5... | collective-permute-start | bytes 294920 | tf_op jit(solution)/shard_map/ppermute | solution.py:207
  7.1 1.5 %collective-permute-start.2 = (f32[3,32,256]{2,1,0:T(8,128)}, f32[3,32,256]{2,1,0:T(8,128)S(1)}, u32[]{:S(2)}, u32[]{:S(2)}) collective-permute-start(f32[3,32,256]{2,1,0:T(8,128)} %cols_ref.1), channel_id=1, source_target_pairs={{0,16},{4,20},{8,24},{12,28},{16,0},{20,4},{24,8},{28,12},{1,17},{... | collective-permute-start | bytes 294920 | tf_op jit(solution)/shard_map/ppermute | solution.py:207
  8.6 0.5 %collective-permute-start.5 = (f32[32,64]{1,0:T(8,128)}, f32[32,64]{1,0:T(8,128)S(1)}, u32[]{:S(2)}, u32[]{:S(2)}) collective-permute-start(f32[32,64]{1,0:T(8,128)} %bitcast.2), channel_id=1, source_target_pairs={{0,8},{4,12},{8,0},{12,4},{16,24},{20,28},{24,16},{28,20},{1,9},{5... | collective-permute-start | bytes 24584 | tf_op jit(solution)/shard_map/ppermute | solution.py:207
  9.2 0.7 %copy-done.2 = f32[64,32]{0,1:T(8,128)S(1)} copy-done((f32[64,32]{0,1:T(8,128)S(1)}, f32[64,32]{0,1:T(8,128)}, u32[]{:S(2)}) %copy-start.2) | copy-done | bytes 8216
  9.9 0.1 vectors.1.extra_ref
  10.0 0.0 collective-permute-done.1.far_ref
  10.0 0.6 %collective-permute-done.cols_ref = f32[3,32,256]{2,1,0:T(8,128)S(1)} collective-permute-done((f32[3,32,256]{2,1,0:T(8,128)}, f32[3,32,256]{2,1,0:T(8,128)S(1)}, u32[]{:S(2)}, u32[]{:S(2)}) %collective-permute-start) | collective-permute-done | bytes 98336 | tf_op jit(solution)/shard_map/ppermute | solution.py:207
  10.6 0.1 after_first.1
  10.7 1.4 %collective-permute-start.4 = (f32[104,256]{1,0:T(8,128)S(1)}, f32[104,256]{1,0:T(8,128)S(1)}, u32[]{:S(2)}, u32[]{:S(2)}) collective-permute-start(f32[104,256]{1,0:T(8,128)S(1)} %get-tuple-element.20.sent_ref), channel_id=1, source_target_pairs={{0,16},{4,20},{8,24},{12,28},{16,0},{20,4},{24,8},{28,12},{1,17},{... | collective-permute-start | bytes 319496 | tf_op jit(solution)/shard_map/ppermute | solution.py:207
  12.1 0.5 %collective-permute-done.5.first_vec_ref = f32[32,64]{1,0:T(8,128)S(1)} collective-permute-done((f32[32,64]{1,0:T(8,128)}, f32[32,64]{1,0:T(8,128)S(1)}, u32[]{:S(2)}, u32[]{:S(2)}) %collective-permute-start.5) | collective-permute-done | bytes 8224 | tf_op jit(solution)/shard_map/ppermute | solution.py:207
  12.6 0.5 %collective-permute-start.6 = (f32[32,64]{1,0:T(8,128)S(1)}, f32[32,64]{1,0:T(8,128)S(1)}, u32[]{:S(2)}, u32[]{:S(2)}) collective-permute-start(f32[32,64]{1,0:T(8,128)S(1)} %collective-permute-done.5.first_vec_ref), channel_id=1, source_target_pairs={{0,16},{4,20},{8,24},{12,28},{16,0},{20,4},{24,8},{28,12},{1,17},{... | collective-permute-start | bytes 24584 | tf_op jit(solution)/shard_map/ppermute | solution.py:207
  13.1 0.4 %collective-permute-start.7 = (f32[3,32,256]{2,1,0:T(8,128)S(1)}, f32[3,32,256]{2,1,0:T(8,128)S(1)}, u32[]{:S(2)}, u32[]{:S(2)}) collective-permute-start(f32[3,32,256]{2,1,0:T(8,128)S(1)} %get-tuple-element.18.after_ref.far_ref), channel_id=1, source_target_pairs={{0,1},{1,0},{2,3},{3,2},{4,5},{5,4},{6,7},{7,6},{8,9},{9,8},{10,11... | collective-permute-start | bytes 294920 | tf_op jit(solution)/shard_map/ppermute | solution.py:207
  13.5 0.0 collective-permute-done.3.near_ref
  13.5 0.0 collective-permute-done.2.second_cols_ref
  13.6 0.1 own.1
  13.7 2.7 %collective-permute-done.6.both_vec_ref = f32[32,64]{1,0:T(8,128)S(1)} collective-permute-done((f32[32,64]{1,0:T(8,128)S(1)}, f32[32,64]{1,0:T(8,128)S(1)}, u32[]{:S(2)}, u32[]{:S(2)}) %collective-permute-start.6) | collective-permute-done | bytes 8224 | tf_op jit(solution)/shard_map/ppermute | solution.py:207
  16.3 1.4 %collective-permute-done.7.both_ref = f32[3,32,256]{2,1,0:T(8,128)S(1)} collective-permute-done((f32[3,32,256]{2,1,0:T(8,128)S(1)}, f32[3,32,256]{2,1,0:T(8,128)S(1)}, u32[]{:S(2)}, u32[]{:S(2)}) %collective-permute-start.7) | collective-permute-done | bytes 98336 | tf_op jit(solution)/shard_map/ppermute | solution.py:207
  17.7 0.0 collective-permute-done.4.got_ref
  17.7 0.1 after_second.1
  17.8 0.1 collective-permute-start.8
  17.9 1.2 %first_tile.1 = (f32[1,128,128]{2,1,0:T(8,128)S(1)}, bf16[1,384,768]{2,1,0:T(8,128)(2,1)S(1)}, f32[1,128,128]{2,1,0:T(8,128)S(1)}) custom-call(f32[4,3,32,256]{3,2,1,0:T(8,128)S(1)} %get-tuple-element.22.rows_ref, f32[4,104,256]{2,1,0:T(8,128)S(1)} %get-tuple-element.23.blocks_ref), custom_call_target="tpu_custom_call" | custom-call | flops 226492416 | bytes 819200 | tf_op jit(solution)/shard_map/first_tile/pallas_call | solution.py:213
  19.1 0.5 %collective-permute-done.8.blocks_ref = f32[4,104,256]{2,1,0:T(8,128)S(1)} collective-permute-done((f32[4,104,256]{2,1,0:T(8,128)S(1)}, f32[4,104,256]{2,1,0:T(8,128)S(1)}, u32[]{:S(2)}, u32[]{:S(2)}) %collective-permute-start.8) | collective-permute-done | bytes 426016 | tf_op jit(solution)/shard_map/ppermute | solution.py:207
  19.6 1.2 %second_tile.1 = (f32[32,128]{1,0:T(8,128)S(1)}, f32[32,128]{1,0:T(8,128)S(1)}, f32[32,128]{1,0:T(8,128)S(1)}, f32[32,128]{1,0:T(8,128)S(1)}) custom-call(f32[1,128,128]{2,1,0:T(8,128)S(1)} %get-tuple-element.24.sum_ref, bf16[1,384,768]{2,1,0:T(8,128)(2,1)S(1)} %get-tuple-element.25.side_ref, f32[1,128,128]{2,1,0:T(8,128)S(1)} %get-tuple-element.26.norm_ref, ...), custom_call_target="tpu_custom_call" | custom-call | flops 226492416 | bytes 1736704 | tf_op jit(solution)/shard_map/second_tile/pallas_call | solution.py:213
  20.9 1.9 %collective-permute-start.9 = (f32[32,128]{1,0:T(8,128)S(1)}, f32[32,128]{1,0:T(8,128)S(1)}, u32[]{:S(2)}, u32[]{:S(2)}) collective-permute-start(f32[32,128]{1,0:T(8,128)S(1)} %get-tuple-element.28), channel_id=1, source_target_pairs={{0,3},{1,2},{2,1},{3,0},{4,7},{5,6},{6,5},{7,4},{8,11},{9,10},{10,... | collective-permute-start | bytes 49160 | tf_op jit(solution)/shard_map/ppermute | solution.py:207
  22.7 0.1 collective-permute-start.10
  22.9 2.5 %collective-permute-start.11 = (f32[32,128]{1,0:T(8,128)S(1)}, f32[32,128]{1,0:T(8,128)S(1)}, u32[]{:S(2)}, u32[]{:S(2)}) collective-permute-start(f32[32,128]{1,0:T(8,128)S(1)} %get-tuple-element.30), channel_id=1, source_target_pairs={{0,1},{1,0},{2,3},{3,2},{4,5},{5,4},{6,7},{7,6},{8,9},{9,8},{10,11... | collective-permute-start | bytes 49160 | tf_op jit(solution)/shard_map/ppermute | solution.py:207
  25.3 1.1 %collective-permute-done.9.refs_1_ = f32[32,128]{1,0:T(8,128)S(1)} collective-permute-done((f32[32,128]{1,0:T(8,128)S(1)}, f32[32,128]{1,0:T(8,128)S(1)}, u32[]{:S(2)}, u32[]{:S(2)}) %collective-permute-start.9) | collective-permute-done | bytes 16416 | tf_op jit(solution)/shard_map/ppermute | solution.py:207
  26.5 0.9 %collective-permute-done.10.refs_2_ = f32[32,128]{1,0:T(8,128)S(1)} collective-permute-done((f32[32,128]{1,0:T(8,128)S(1)}, f32[32,128]{1,0:T(8,128)S(1)}, u32[]{:S(2)}, u32[]{:S(2)}) %collective-permute-start.10) | collective-permute-done | bytes 16416 | tf_op jit(solution)/shard_map/ppermute | solution.py:207
  27.4 0.0 collective-permute-done.11.refs_3_
  27.4 0.7 %sum_divide.1 = f32[32,64]{1,0:T(8,128)} custom-call(f32[32,128]{1,0:T(8,128)S(1)} %get-tuple-element.27.refs_0_, f32[32,128]{1,0:T(8,128)S(1)} %collective-permute-done.9.refs_1_, f32[32,128]{1,0:T(8,128)S(1)} %collective-permute-done.10.refs_2_, f32[32,128]{1,0:T(8,128)S(1)} %collective-permute-done.11.refs_3_), custom_call_target="tpu_custom_call" | custom-call | bytes 65536 | tf_op jit(solution)/shard_map/sum_divide/pallas_call | solution.py:213
  (5 shorter events, 0.0 us)
Async XLA Ops:
  0.0 10.0 %collective-permute-start.1 = (f32[3,32,256]{2,1,0:T(8,128)}, f32[3,32,256]{2,1,0:T(8,128)S(1)}, u32[]{:S(2)}, u32[]{:S(2)}) collective-permute-start(f32[3,32,256]{2,1,0:T(8,128)} %rows_ref.1), channel_id=1, source_target_pairs={{0,2},{1,3},{2,0},{3,1},{4,6},{5,7},{6,4},{7,5},{8,10},{9,11},{10,... | collective-permute-start | bytes 294920 | tf_op jit(solution)/shard_map/ppermute | solution.py:207
  4.0 9.5 %collective-permute-start.3 = (f32[3,32,256]{2,1,0:T(8,128)}, f32[3,32,256]{2,1,0:T(8,128)S(1)}, u32[]{:S(2)}, u32[]{:S(2)}) collective-permute-start(f32[3,32,256]{2,1,0:T(8,128)} %rows_ref.1), channel_id=1, source_target_pairs={{0,1},{1,0},{2,3},{3,2},{4,5},{5,4},{6,7},{7,6},{8,9},{9,8},{10,11... | collective-permute-start | bytes 294920 | tf_op jit(solution)/shard_map/ppermute | solution.py:207
  5.6 5.0 %collective-permute-start = (f32[3,32,256]{2,1,0:T(8,128)}, f32[3,32,256]{2,1,0:T(8,128)S(1)}, u32[]{:S(2)}, u32[]{:S(2)}) collective-permute-start(f32[3,32,256]{2,1,0:T(8,128)} %cols_ref.1), channel_id=1, source_target_pairs={{0,8},{4,12},{8,0},{12,4},{16,24},{20,28},{24,16},{28,20},{1,9},{5... | collective-permute-start | bytes 294920 | tf_op jit(solution)/shard_map/ppermute | solution.py:207
  7.1 6.4 %collective-permute-start.2 = (f32[3,32,256]{2,1,0:T(8,128)}, f32[3,32,256]{2,1,0:T(8,128)S(1)}, u32[]{:S(2)}, u32[]{:S(2)}) collective-permute-start(f32[3,32,256]{2,1,0:T(8,128)} %cols_ref.1), channel_id=1, source_target_pairs={{0,16},{4,20},{8,24},{12,28},{16,0},{20,4},{24,8},{28,12},{1,17},{... | collective-permute-start | bytes 294920 | tf_op jit(solution)/shard_map/ppermute | solution.py:207
  8.6 3.9 %collective-permute-start.5 = (f32[32,64]{1,0:T(8,128)}, f32[32,64]{1,0:T(8,128)S(1)}, u32[]{:S(2)}, u32[]{:S(2)}) collective-permute-start(f32[32,64]{1,0:T(8,128)} %bitcast.2), channel_id=1, source_target_pairs={{0,8},{4,12},{8,0},{12,4},{16,24},{20,28},{24,16},{28,20},{1,9},{5... | collective-permute-start | bytes 24584 | tf_op jit(solution)/shard_map/ppermute | solution.py:207
  9.2 0.8 %copy-start.2 = (f32[64,32]{0,1:T(8,128)S(1)}, f32[64,32]{0,1:T(8,128)}, u32[]{:S(2)}) copy-start(f32[64,32]{0,1:T(8,128)} %param.5) | copy-start | bytes 24580
  10.0 3.6 %copy-start = (f32[3,32,256]{2,1,0:T(8,128)S(1)}, f32[3,32,256]{2,1,0:T(8,128)}, u32[]{:S(2)}) copy-start(f32[3,32,256]{2,1,0:T(8,128)} %rows_ref.1) | copy-start | bytes 294916
  10.0 3.6 %copy-start.1 = (f32[3,32,256]{2,1,0:T(8,128)S(1)}, f32[3,32,256]{2,1,0:T(8,128)}, u32[]{:S(2)}) copy-start(f32[3,32,256]{2,1,0:T(8,128)} %cols_ref.1) | copy-start | bytes 294916
  10.7 7.0 %collective-permute-start.4 = (f32[104,256]{1,0:T(8,128)S(1)}, f32[104,256]{1,0:T(8,128)S(1)}, u32[]{:S(2)}, u32[]{:S(2)}) collective-permute-start(f32[104,256]{1,0:T(8,128)S(1)} %get-tuple-element.20.sent_ref), channel_id=1, source_target_pairs={{0,16},{4,20},{8,24},{12,28},{16,0},{20,4},{24,8},{28,12},{1,17},{... | collective-permute-start | bytes 319496 | tf_op jit(solution)/shard_map/ppermute | solution.py:207
  12.6 3.7 %collective-permute-start.6 = (f32[32,64]{1,0:T(8,128)S(1)}, f32[32,64]{1,0:T(8,128)S(1)}, u32[]{:S(2)}, u32[]{:S(2)}) collective-permute-start(f32[32,64]{1,0:T(8,128)S(1)} %collective-permute-done.5.first_vec_ref), channel_id=1, source_target_pairs={{0,16},{4,20},{8,24},{12,28},{16,0},{20,4},{24,8},{28,12},{1,17},{... | collective-permute-start | bytes 24584 | tf_op jit(solution)/shard_map/ppermute | solution.py:207
  13.1 4.6 %collective-permute-start.7 = (f32[3,32,256]{2,1,0:T(8,128)S(1)}, f32[3,32,256]{2,1,0:T(8,128)S(1)}, u32[]{:S(2)}, u32[]{:S(2)}) collective-permute-start(f32[3,32,256]{2,1,0:T(8,128)S(1)} %get-tuple-element.18.after_ref.far_ref), channel_id=1, source_target_pairs={{0,1},{1,0},{2,3},{3,2},{4,5},{5,4},{6,7},{7,6},{8,9},{9,8},{10,11... | collective-permute-start | bytes 294920 | tf_op jit(solution)/shard_map/ppermute | solution.py:207
  17.8 1.8 %collective-permute-start.8 = (f32[4,104,256]{2,1,0:T(8,128)S(1)}, f32[4,104,256]{2,1,0:T(8,128)S(1)}, u32[]{:S(2)}, u32[]{:S(2)}) collective-permute-start(f32[4,104,256]{2,1,0:T(8,128)S(1)} %get-tuple-element.23.blocks_ref), channel_id=1, source_target_pairs={{0,4},{4,0},{8,12},{12,8},{16,20},{20,16},{24,28},{28,24},{1,5},{5... | collective-permute-start | bytes 1277960 | tf_op jit(solution)/shard_map/ppermute | solution.py:207
  20.9 5.6 %collective-permute-start.9 = (f32[32,128]{1,0:T(8,128)S(1)}, f32[32,128]{1,0:T(8,128)S(1)}, u32[]{:S(2)}, u32[]{:S(2)}) collective-permute-start(f32[32,128]{1,0:T(8,128)S(1)} %get-tuple-element.28), channel_id=1, source_target_pairs={{0,3},{1,2},{2,1},{3,0},{4,7},{5,6},{6,5},{7,4},{8,11},{9,10},{10,... | collective-permute-start | bytes 49160 | tf_op jit(solution)/shard_map/ppermute | solution.py:207
  22.7 4.6 %collective-permute-start.10 = (f32[32,128]{1,0:T(8,128)S(1)}, f32[32,128]{1,0:T(8,128)S(1)}, u32[]{:S(2)}, u32[]{:S(2)}) collective-permute-start(f32[32,128]{1,0:T(8,128)S(1)} %get-tuple-element.29), channel_id=1, source_target_pairs={{0,2},{1,3},{2,0},{3,1},{4,6},{5,7},{6,4},{7,5},{8,10},{9,11},{10,... | collective-permute-start | bytes 49160 | tf_op jit(solution)/shard_map/ppermute | solution.py:207
  22.9 4.5 %collective-permute-start.11 = (f32[32,128]{1,0:T(8,128)S(1)}, f32[32,128]{1,0:T(8,128)S(1)}, u32[]{:S(2)}, u32[]{:S(2)}) collective-permute-start(f32[32,128]{1,0:T(8,128)S(1)} %get-tuple-element.30), channel_id=1, source_target_pairs={{0,1},{1,0},{2,3},{3,2},{4,5},{5,4},{6,7},{7,6},{8,9},{9,8},{10,11... | collective-permute-start | bytes 49160 | tf_op jit(solution)/shard_map/ppermute | solution.py:207
